TPU v7x, 32 devices: a whole 2x2x4 slice. The times are simulated.
32 devices in a mesh: freq: 8 (over z, core), src: 4 (over y, x).
Axes of the slice: x: 2, y: 2, z: 4, core: 2. Of those that a mesh axis runs over, the one named last changes fastest.
Arguments:
- reflection: bfloat16 [8, 2, 6400, 6400], P('freq', None, 'src'), may hold values from -0.078125 to 0.078125
- f_zero: float32 [8, 2, 16, 6400], P('freq'), may hold values from -6 to 6
- onset: int32 [16, 6400], replicated, may hold values from 64 to 447
Outputs:
- f_plus: float32 [8, 2, 16, 6400], P('freq')
- f_minus: float32 [8, 2, 16, 6400], P('freq', None, None, 'src')
All inputs are finite; a program needn't handle non-finite values.
Results may differ from a plain program's by a relative error of at most 0.013.
Values may be sent and summed in bfloat16 or wider, within the bound.
A program may use at most 192 MiB of HBM per device.

v0:
```python
import math

import jax
import jax.numpy as jnp
from jax import lax
from jax.sharding import PartitionSpec as P

SAMPLES = 512
LOW_BIN = 4
ROUNDS = 5


def band_table(count, samples):
    bins = lax.broadcasted_iota(jnp.int32, (count, samples), 0) + (LOW_BIN + 1)
    moments = lax.broadcasted_iota(jnp.int32, (count, samples), 1)
    phase = (bins * moments % samples).astype(jnp.float32) * (2.0 * math.pi / samples)
    factor = math.sqrt(2.0 / samples)
    return jnp.stack([factor * jnp.cos(phase), -factor * jnp.sin(phase)], axis=1).reshape(
        2 * count, samples
    )


def windowed(spectra, onset_cols, table):
    count, parts, virt, width = spectra.shape
    flat = spectra.reshape(count * parts, virt * width)
    traces = jnp.einsum("an,at->nt", flat, table, precision=lax.Precision.HIGHEST)
    moments = lax.broadcasted_iota(jnp.int32, traces.shape, 1)
    kept = jnp.where(moments < onset_cols.reshape(virt * width, 1), traces, jnp.zeros_like(traces))
    back = jnp.einsum("at,nt->an", table, kept, precision=lax.Precision.HIGHEST)
    return back.reshape(count, parts, virt, width)


def forward_product(plus_b, reflection):
    prod = jnp.einsum("favr,fbsr->fabvs", plus_b, reflection, preferred_element_type=jnp.float32)
    real = prod[:, 0, 0] - prod[:, 1, 1]
    imag = prod[:, 1, 0] + prod[:, 0, 1]
    return jnp.stack([real, imag], axis=1)


def adjoint_product(minus_b, reflection):
    prod = jnp.einsum("favs,fbsr->fabvr", minus_b, reflection, preferred_element_type=jnp.float32)
    real = prod[:, 0, 0] + prod[:, 1, 1]
    imag = prod[:, 1, 0] - prod[:, 0, 1]
    return jnp.stack([real, imag], axis=1)


def body(reflection, f_zero, onset):
    n_freq = lax.axis_size("freq")
    freq_index = lax.axis_index("freq")
    src_index = lax.axis_index("src")
    local_freqs = reflection.shape[0]
    src_rows = reflection.shape[2]
    points = reflection.shape[3]
    table = band_table(local_freqs * n_freq, SAMPLES)
    src_piece = src_rows // n_freq
    src_start = src_index * src_rows + freq_index * src_piece
    onset_src = lax.dynamic_slice_in_dim(onset, src_start, src_piece, 1)
    recv_piece = points // n_freq
    recv_start = freq_index * recv_piece
    onset_recv = lax.dynamic_slice_in_dim(onset, recv_start, recv_piece, 1)
    plus = f_zero
    minus = None
    for step in range(ROUNDS):
        records = forward_product(plus.astype(jnp.bfloat16), reflection)
        spread = lax.all_to_all(records, "freq", split_axis=3, concat_axis=0, tiled=True)
        upgoing = windowed(spread, onset_src, table)
        if step + 1 < ROUNDS:
            minus_b = lax.all_to_all(
                upgoing.astype(jnp.bfloat16), "freq", split_axis=0, concat_axis=3, tiled=True
            )
        else:
            minus = lax.all_to_all(
                upgoing.astype(jnp.bfloat16), "freq", split_axis=0, concat_axis=3, tiled=True
            ).astype(upgoing.dtype)
            minus_b = minus.astype(jnp.bfloat16)
        partial_sum = adjoint_product(minus_b, reflection)
        total = lax.psum(partial_sum.astype(jnp.bfloat16), "src").astype(jnp.float32)
        cut_total = lax.all_to_all(total, "freq", split_axis=3, concat_axis=0, tiled=True)
        correction = lax.all_to_all(
            windowed(cut_total, onset_recv, table), "freq", split_axis=0, concat_axis=3, tiled=True
        )
        plus = f_zero + correction
    return (plus, minus)


def solution(mesh):
    return jax.shard_map(
        body,
        mesh=mesh,
        in_specs=(P("freq", None, "src", None), P("freq", None, None, None), P()),
        out_specs=(P("freq", None, None, None), P("freq", None, None, "src")),
        check_vma=False,
    )
```

profile of v0, /device:TPU:0, one launch (start us, length us, event | category | flops | bytes accessed | tf_op | source)
XLA Modules:
  0.0 1363.4 jit_solution(1645985463577592683)
XLA Ops:
  89.5 43.5 %all-reduce.6.cloned.1.call-done = bf16[1,2,16,6400]{3,2,1,0:T(8,128)(2,1)} async-done(((bf16[1,2,16,6400]{3,2,1,0:T(8,128)(2,1)}), bf16[1,2,16,6400]{3,2,1,0:T(8,128)(2,1)}) %all-reduce.6.cloned.1.call-update) | async-done | bytes 409616 | tf_op jit(solution)/shard_map/psum | solution.py:77
  201.0 26.1 %fusion.24 = f32[12800,512]{1,0:T(8,128)} fusion(f32[16,12800]{1,0:T(8,128)S(1)} %reshape.986, f32[16,512]{1,0:T(8,128)S(1)} %reshape.984, s32[12800]{0:T(1024)S(1)} %lt.26), kind=kOutput, calls=%fused_computation.25 | convolution fusion | flops 1271398400 | bytes 27117568 | tf_op jit(solution)/shard_map/an,at->nt/dot_general | solution.py:26
  227.1 25.5 %fusion.113 = f32[8,2,16,800]{3,0,2,1:T(8,128)S(1)} fusion(f32[16,800,512,1]{2,1,0,3:T(8,128)} %bitcast.412, f32[8,1,512]{2,0,1:T(8,128)S(1)} %get-tuple-element.21, f32[8,1,512]{2,0,1:T(8,128)S(1)} %get-tuple-element.20), kind=kOutput, calls=%fused_computation.137 | convolution fusion | flops 1258299392 | bytes 27066368 | tf_op jit(solution)/shard_map/at,nt->an/dot_general | solution.py:29
  252.8 26.7 %all_to_all.316 = f32[8,2,16,800]{3,2,1,0:T(8,128)S(1)} all-to-all(f32[8,2,16,800]{3,2,1,0:T(8,128)S(1)} %copy.67), channel_id=1, replica_groups=mesh['freq'=8,'src'=4] {'freq'}, dimensions={0} | all-to-all | bytes 1638400 | tf_op jit(solution)/shard_map/all_to_all | solution.py:79
  358.0 42.6 %all-reduce.8.cloned.1.call-done = bf16[1,2,16,6400]{3,2,1,0:T(8,128)(2,1)} async-done(((bf16[1,2,16,6400]{3,2,1,0:T(8,128)(2,1)}), bf16[1,2,16,6400]{3,2,1,0:T(8,128)(2,1)}) %all-reduce.8.cloned.1.call-update) | async-done | bytes 409616 | tf_op jit(solution)/shard_map/psum | solution.py:77
  418.3 26.1 %all_to_all.319 = f32[8,1,25600]{2,1,0:T(1,128)S(1)} all-to-all(f32[8,1,25600]{2,1,0:T(1,128)S(1)} %reshape.1037), channel_id=1, replica_groups=mesh['freq'=8,'src'=4] {'freq'}, dimensions={0} | all-to-all | bytes 1638400 | tf_op jit(solution)/shard_map/all_to_all | solution.py:78
  468.4 27.3 %fusion.23 = f32[12800,512]{1,0:T(8,128)} fusion(f32[16,12800]{1,0:T(8,128)} %reshape.990, f32[16,512]{1,0:T(8,128)S(1)} %reshape.984, s32[12800]{0:T(1024)S(1)} %lt.26), kind=kOutput, calls=%fused_computation.24 | convolution fusion | flops 1271398400 | bytes 27117568 | tf_op jit(solution)/shard_map/an,at->nt/dot_general | solution.py:26
  495.7 25.5 %fusion.110 = f32[8,2,16,800]{3,0,2,1:T(8,128)S(1)} fusion(f32[16,800,512,1]{2,1,0,3:T(8,128)} %bitcast.413, f32[8,1,512]{2,0,1:T(8,128)S(1)} %get-tuple-element.21, f32[8,1,512]{2,0,1:T(8,128)S(1)} %get-tuple-element.20), kind=kOutput, calls=%fused_computation.134 | convolution fusion | flops 1258299392 | bytes 27066368 | tf_op jit(solution)/shard_map/at,nt->an/dot_general | solution.py:29
  521.4 26.4 %all_to_all.320 = f32[8,2,16,800]{3,2,1,0:T(8,128)S(1)} all-to-all(f32[8,2,16,800]{3,2,1,0:T(8,128)S(1)} %copy.75), channel_id=1, replica_groups=mesh['freq'=8,'src'=4] {'freq'}, dimensions={0} | all-to-all | bytes 1638400 | tf_op jit(solution)/shard_map/all_to_all | solution.py:79
  626.5 42.6 %all-reduce.10.cloned.1.call-done = bf16[1,2,16,6400]{3,2,1,0:T(8,128)(2,1)} async-done(((bf16[1,2,16,6400]{3,2,1,0:T(8,128)(2,1)}), bf16[1,2,16,6400]{3,2,1,0:T(8,128)(2,1)}) %all-reduce.10.cloned.1.call-update) | async-done | bytes 409616 | tf_op jit(solution)/shard_map/psum | solution.py:77
  686.8 26.1 %all_to_all.323 = f32[8,1,25600]{2,1,0:T(1,128)S(1)} all-to-all(f32[8,1,25600]{2,1,0:T(1,128)S(1)} %reshape.1041), channel_id=1, replica_groups=mesh['freq'=8,'src'=4] {'freq'}, dimensions={0} | all-to-all | bytes 1638400 | tf_op jit(solution)/shard_map/all_to_all | solution.py:78
  736.9 27.1 %fusion.22 = f32[12800,512]{1,0:T(8,128)} fusion(f32[16,12800]{1,0:T(8,128)} %reshape.994, f32[16,512]{1,0:T(8,128)S(1)} %reshape.984, s32[12800]{0:T(1024)S(1)} %lt.26), kind=kOutput, calls=%fused_computation.23 | convolution fusion | flops 1271398400 | bytes 27117568 | tf_op jit(solution)/shard_map/an,at->nt/dot_general | solution.py:26
  764.0 25.5 %fusion.107 = f32[8,2,16,800]{3,0,2,1:T(8,128)S(1)} fusion(f32[16,800,512,1]{2,1,0,3:T(8,128)} %bitcast.414, f32[8,1,512]{2,0,1:T(8,128)S(1)} %get-tuple-element.21, f32[8,1,512]{2,0,1:T(8,128)S(1)} %get-tuple-element.20), kind=kOutput, calls=%fused_computation.131 | convolution fusion | flops 1258299392 | bytes 27066368 | tf_op jit(solution)/shard_map/at,nt->an/dot_general | solution.py:29
  789.7 26.4 %all_to_all.324 = f32[8,2,16,800]{3,2,1,0:T(8,128)S(1)} all-to-all(f32[8,2,16,800]{3,2,1,0:T(8,128)S(1)} %copy.83), channel_id=1, replica_groups=mesh['freq'=8,'src'=4] {'freq'}, dimensions={0} | all-to-all | bytes 1638400 | tf_op jit(solution)/shard_map/all_to_all | solution.py:79
  894.8 42.6 %all-reduce.12.cloned.1.call-done = bf16[1,2,16,6400]{3,2,1,0:T(8,128)(2,1)} async-done(((bf16[1,2,16,6400]{3,2,1,0:T(8,128)(2,1)}), bf16[1,2,16,6400]{3,2,1,0:T(8,128)(2,1)}) %all-reduce.12.cloned.1.call-update) | async-done | bytes 409616 | tf_op jit(solution)/shard_map/psum | solution.py:77
  955.1 26.1 %all_to_all.327 = f32[8,1,25600]{2,1,0:T(1,128)S(1)} all-to-all(f32[8,1,25600]{2,1,0:T(1,128)S(1)} %reshape.1045), channel_id=1, replica_groups=mesh['freq'=8,'src'=4] {'freq'}, dimensions={0} | all-to-all | bytes 1638400 | tf_op jit(solution)/shard_map/all_to_all | solution.py:78
  1005.2 27.1 %fusion.21 = f32[12800,512]{1,0:T(8,128)} fusion(f32[16,12800]{1,0:T(8,128)} %reshape.998, f32[16,512]{1,0:T(8,128)S(1)} %reshape.984, s32[12800]{0:T(1024)S(1)} %lt.26), kind=kOutput, calls=%fused_computation.22 | convolution fusion | flops 1271398400 | bytes 27117568 | tf_op jit(solution)/shard_map/an,at->nt/dot_general | solution.py:26
  1032.3 25.5 %fusion.104 = f32[8,2,16,800]{3,0,2,1:T(8,128)S(1)} fusion(f32[16,800,512,1]{2,1,0,3:T(8,128)} %bitcast.415, f32[8,1,512]{2,0,1:T(8,128)S(1)} %get-tuple-element.21, f32[8,1,512]{2,0,1:T(8,128)S(1)} %get-tuple-element.20), kind=kOutput, calls=%fused_computation.128 | convolution fusion | flops 1258299392 | bytes 27066368 | tf_op jit(solution)/shard_map/at,nt->an/dot_general | solution.py:29
  1058.0 26.6 %all_to_all.328 = f32[8,2,16,800]{3,2,1,0:T(8,128)S(1)} all-to-all(f32[8,2,16,800]{3,2,1,0:T(8,128)S(1)} %copy.91), channel_id=1, replica_groups=mesh['freq'=8,'src'=4] {'freq'}, dimensions={0} | all-to-all | bytes 1638400 | tf_op jit(solution)/shard_map/all_to_all | solution.py:79
  1163.1 42.6 %all-reduce.14.cloned.1.call-done = bf16[1,2,16,6400]{3,2,1,0:T(8,128)(2,1)} async-done(((bf16[1,2,16,6400]{3,2,1,0:T(8,128)(2,1)}), bf16[1,2,16,6400]{3,2,1,0:T(8,128)(2,1)}) %all-reduce.14.cloned.1.call-update) | async-done | bytes 409616 | tf_op jit(solution)/shard_map/psum | solution.py:77
  1223.4 26.1 %all_to_all.331 = f32[8,1,25600]{2,1,0:T(1,128)S(1)} all-to-all(f32[8,1,25600]{2,1,0:T(1,128)S(1)} %reshape.1049), channel_id=1, replica_groups=mesh['freq'=8,'src'=4] {'freq'}, dimensions={0} | all-to-all | bytes 1638400 | tf_op jit(solution)/shard_map/all_to_all | solution.py:78
  1273.5 27.1 %fusion.20 = f32[12800,512]{1,0:T(8,128)} fusion(f32[16,12800]{1,0:T(8,128)} %reshape.1002, f32[16,512]{1,0:T(8,128)S(1)} %reshape.984, s32[12800]{0:T(1024)S(1)} %lt.26), kind=kOutput, calls=%fused_computation.21 | convolution fusion | flops 1271398400 | bytes 27117568 | tf_op jit(solution)/shard_map/an,at->nt/dot_general | solution.py:26
  1300.6 25.6 %fusion.101 = f32[8,2,16,800]{3,0,2,1:T(8,128)S(1)} fusion(f32[16,800,512,1]{2,1,0,3:T(8,128)} %bitcast.411, f32[8,1,512]{2,0,1:T(8,128)S(1)} %get-tuple-element.21, f32[8,1,512]{2,0,1:T(8,128)S(1)} %get-tuple-element.20), kind=kOutput, calls=%fused_computation.125 | convolution fusion | flops 1258299392 | bytes 27066368 | tf_op jit(solution)/shard_map/at,nt->an/dot_general | solution.py:29
  1331.9 22.7 %all-to-all-done.19 = f32[8,2,16,800]{3,2,1,0:T(8,128)S(1)} async-done(((f32[8,2,16,800]{3,2,1,0:T(8,128)}), f32[8,2,16,800]{3,2,1,0:T(8,128)S(1)}, u32[]{:S(2)}, u32[]{:S(2)}) %all-to-all-start.19) | async-done | bytes 819232 | tf_op jit(solution)/shard_map/all_to_all | solution.py:79
  (175 shorter events, 639.1 us)
Async XLA Ops:
  7.2 30.3 %copy-start = (s32[16,6400]{1,0:T(8,128)S(1)}, s32[16,6400]{1,0:T(8,128)}, u32[]{:S(2)}) copy-start(s32[16,6400]{1,0:T(8,128)} %param.5) | copy-start | bytes 1228804
  30.8 14.8 %all-to-all-start = ((f32[8,1,6400]{2,1,0:T(1,128)}), f32[8,1,6400]{2,1,0:T(1,128)S(1)}, u32[]{:S(2)}, u32[]{:S(2)}) async-start(f32[8,1,6400]{2,1,0:T(1,128)} %reshape.1031), calls=%async_computation | async-start | bytes 409600 | tf_op jit(solution)/shard_map/all_to_all | solution.py:65
  37.1 95.9 %all-reduce.6.cloned.1.call-start = ((), (), s32[]{:S(2)}) async-start(), calls=%async_computation.20 | async-start | bytes 819200 | tf_op jit(solution)/shard_map/psum | solution.py:77
  151.4 26.3 %all-to-all-start.2 = ((f32[8,1,25600]{2,1,0:T(1,128)}), f32[8,1,25600]{2,1,0:T(1,128)S(1)}, u32[]{:S(2)}, u32[]{:S(2)}) async-start(f32[8,1,25600]{2,1,0:T(1,128)} %reshape.1033), calls=%async_computation.2 | async-start | bytes 1638400 | tf_op jit(solution)/shard_map/all_to_all | solution.py:78
  156.0 244.6 %all-reduce.8.cloned.1.call-start = ((), (), s32[]{:S(2)}) async-start(), calls=%async_computation.21 | async-start | bytes 819200 | tf_op jit(solution)/shard_map/psum | solution.py:77
  252.6 29.8 %copy-start.2 = (f32[1,2,16,6400]{3,2,1,0:T(8,128)S(1)}, f32[1,2,16,6400]{3,2,1,0:T(8,128)}, u32[]{:S(2)}) copy-start(f32[1,2,16,6400]{3,2,1,0:T(8,128)} %param.4) | copy-start | bytes 2457604
  358.0 311.1 %all-reduce.10.cloned.1.call-start = ((), (), s32[]{:S(2)}) async-start(), calls=%async_computation.22 | async-start | bytes 819200 | tf_op jit(solution)/shard_map/psum | solution.py:77
  626.5 310.9 %all-reduce.12.cloned.1.call-start = ((), (), s32[]{:S(2)}) async-start(), calls=%async_computation.23 | async-start | bytes 819200 | tf_op jit(solution)/shard_map/psum | solution.py:77
  894.7 310.9 %all-reduce.14.cloned.1.call-start = ((), (), s32[]{:S(2)}) async-start(), calls=%async_computation.24 | async-start | bytes 819200 | tf_op jit(solution)/shard_map/psum | solution.py:77
  1300.6 55.8 %copy-start.1 = (s32[16,6400]{1,0:T(8,128)S(1)}, s32[16,6400]{1,0:T(8,128)}, u32[]{:S(2)}) copy-start(s32[16,6400]{1,0:T(8,128)} %param.5) | copy-start | bytes 1228804
  1327.3 27.3 %all-to-all-start.19 = ((f32[8,2,16,800]{3,2,1,0:T(8,128)}), f32[8,2,16,800]{3,2,1,0:T(8,128)S(1)}, u32[]{:S(2)}, u32[]{:S(2)}) async-start(f32[8,2,16,800]{3,2,1,0:T(8,128)} %copy.99), calls=%async_computation.19 | async-start | bytes 1835008 | tf_op jit(solution)/shard_map/all_to_all | solution.py:79
Sparse Core Ops, SparseCore 0:
  89.6 43.3 all-reduce.5
  358.1 42.4 all-reduce.7
  626.6 42.4 all-reduce.9
  894.9 42.4 all-reduce.11
  1163.2 42.4 all-reduce.13
where the time goes:
time: 1370 us; the launch traced here: 1360 us
  matrix products  487 us (36%)
  blocking collectives  301 us (22%)
  waiting for transfers between devices  266 us (19%)
  local copies, waits for them, and re-layouts  255 us (19%)
  other arithmetic  24.4 us (2%)
  between operations  15 us (1%)
  starting transfers between devices  14.7 us (1%)
    psum x5, waiting for transfers between devices, body(): lax.psum(partial_sum.astype(jnp.bfloat16), 'src').astype(jnp.float32)  214 us
    dot_general x10, matrix products, windowed(): jnp.einsum('an,at->nt', flat, table, precision=lax.Precision.HIGHEST)  164 us
    dot_general x10, matrix products, windowed(): back = jnp.einsum('at,nt->an', table, kept, precision=lax.Precision.HIGHEST)  155 us
    unnamed x26, local copies, waits for them, and re-layouts  133 us
    all_to_all x4, blocking collectives, body(): lax.all_to_all(windowed(cut_total, onset_recv, table), 'freq', split_axis...  106 us
    all_to_all x4, blocking collectives, body(): lax.all_to_all(total, 'freq', split_axis=3, concat_axis=0, tiled=True)  104 us
    dot_general x5, matrix products, forward_product(): jnp.einsum('favr,fbsr->fabvs', plus_b, reflection, preferred_element_type...  89.3 us
    dot_general x5, matrix products, adjoint_product(): jnp.einsum('favs,fbsr->fabvr', minus_b, reflection, preferred_element_typ...  78.9 us
  transfers between devices with their start and end apart: 8, of which 8 were waited for; matrix products, arithmetic and copies ran while one was open for 0% of the time, Pallas kernels for 0%

commit v1 on v0

v1 whole, which is shorter than its diff:
```python
import functools
import math

import jax
import jax.numpy as jnp
import ml_dtypes
import numpy as np
from jax import lax
from jax.experimental import pallas as pl
from jax.experimental.pallas import tpu as pltpu
from jax.sharding import PartitionSpec as P

SAMPLES = 512
LOW_BIN = 4
ROUNDS = 5
LANES = 128
TILE = 256
MESH = pl.DeviceIdType.MESH


def round_up(value, unit):
    return -(-value // unit) * unit


def starts(total, count, width):
    return [min(width * k, total - width) for k in range(count)]


def band_table(count):
    bins = np.arange(count)[:, None] + (LOW_BIN + 1)
    moments = np.arange(SAMPLES)[None, :]
    phase = (bins * moments % SAMPLES) * (2.0 * math.pi / SAMPLES)
    factor = math.sqrt(2.0 / SAMPLES)
    return np.stack([factor * np.cos(phase), -factor * np.sin(phase)], axis=1).reshape(
        2 * count, SAMPLES
    )


def kernel(
    n_freq,
    n_src,
    refl_hbm,
    zero_ref,
    onset_src_ref,
    onset_recv_ref,
    spread_ref,
    gather_ref,
    plus_ref,
    minus_ref,
    refl,
    lhs,
    mlhs,
    rec,
    acc,
    snd,
    got1,
    got2,
    part_snd,
    got3,
    got4,
    got5,
    piece,
    got6,
    load_sem,
    send_sem,
    recv_sem,
):
    me_f = lax.axis_index("freq")
    me_s = lax.axis_index("src")
    rows, points = refl.shape[1], refl.shape[2]
    two_v = lhs.shape[1]
    virt = two_v // 2
    wide = piece.shape[1]
    narrow = snd.shape[2]
    wide_starts = starts(points, n_src, wide)
    narrow_starts = starts(wide, n_freq, narrow)
    edges = list(range(0, rows, TILE))

    def load(j, start, size):
        return pltpu.make_async_copy(
            refl_hbm.at[0, :, pl.ds(start, size), :],
            refl.at[:, pl.ds(start, size), :],
            load_sem.at[j],
        )

    for j, start in enumerate(edges):
        load(j, start, min(TILE, rows - start)).start()

    barrier = pltpu.get_barrier_semaphore()
    for d in range(1, n_freq):
        pl.semaphore_signal(
            barrier, inc=1, device_id={"freq": lax.rem(me_f + d, n_freq)}, device_id_type=MESH
        )
    for d in range(1, n_src):
        pl.semaphore_signal(
            barrier, inc=1, device_id={"src": lax.rem(me_s + d, n_src)}, device_id_type=MESH
        )
    pl.semaphore_wait(barrier, n_freq + n_src - 2)

    def exchange(phase, axis, count, me, source, target):
        copies = []
        for d in range(1, count):
            peer = lax.rem(me + d, count)
            copy = pltpu.make_async_remote_copy(
                src_ref=source(peer),
                dst_ref=target.at[me],
                send_sem=send_sem.at[phase, d],
                recv_sem=recv_sem.at[phase, d],
                device_id={axis: peer},
                device_id_type=MESH,
            )
            copy.start()
            copies.append(copy)
        target[me] = source(me)[...]
        for copy in copies:
            copy.wait()

    def window(source, onset_ref, target):
        spectra = source[...].reshape(n_freq * two_v, narrow)
        row = lax.broadcasted_iota(jnp.int32, (n_freq * two_v, narrow), 0) % virt
        moment = lax.broadcasted_iota(jnp.int32, (SAMPLES, narrow), 0)

        def one(v, total):
            mine = row == v
            picked = jnp.where(mine, spectra.astype(jnp.float32), 0.0).astype(jnp.bfloat16)
            traces = jnp.dot(spread_ref[...], picked, preferred_element_type=jnp.float32)
            kept = jnp.where(moment < onset_ref[pl.ds(v, 1), :], traces, 0.0).astype(jnp.bfloat16)
            back = jnp.dot(gather_ref[...], kept, preferred_element_type=jnp.float32)
            return jnp.where(mine, back, total)

        total = lax.fori_loop(
            0, virt, one, jnp.zeros((n_freq * two_v, narrow), jnp.float32), unroll=2
        )
        target[...] = total.astype(jnp.bfloat16).reshape(n_freq, two_v, narrow)

    def set_plus(values):
        low = values.astype(jnp.bfloat16)
        lhs[0] = low
        lhs[1, :virt] = (-values[virt:]).astype(jnp.bfloat16)
        lhs[1, virt:] = values[:virt].astype(jnp.bfloat16)

    set_plus(zero_ref[0].reshape(two_v, points))
    rec[...] = jnp.zeros_like(rec)

    def forward(start, size):
        out = None
        for p in range(2):
            term = lax.dot_general(
                lhs[p],
                refl[p, pl.ds(start, size), :],
                (((1,), (1,)), ((), ())),
                preferred_element_type=jnp.float32,
            )
            out = term if out is None else out + term
        return out

    def round_body(step, carry):
        full = rows // TILE

        def forward_tile(j, c):
            start = pl.multiple_of(j * TILE, TILE)

            @pl.when(step == 0)
            def _():
                load(j, start, TILE).wait()

            rec[:, pl.ds(start, TILE)] = forward(start, TILE)
            return c

        lax.fori_loop(0, full, forward_tile, 0)
        if rows % TILE:
            start, size = full * TILE, rows % TILE

            @pl.when(step == 0)
            def _():
                load(full, start, size).wait()

            rec[:, start : start + size] = forward(start, size)
        for k in range(n_freq):
            at = narrow_starts[k]
            snd[k] = rec[:, at : at + narrow].astype(jnp.bfloat16)
        exchange(0, "freq", n_freq, me_f, lambda k: snd.at[k], got1)
        window(got1, onset_src_ref, snd)
        exchange(1, "freq", n_freq, me_f, lambda k: snd.at[k], got2)
        for k in range(n_freq):
            at = narrow_starts[k]
            block = got2[k]
            mlhs[0, :, at : at + narrow] = block
            value = block.astype(jnp.float32)
            mlhs[1, :virt, at : at + narrow] = block[virt:]
            mlhs[1, virt:, at : at + narrow] = (-value[:virt]).astype(jnp.bfloat16)
        minus_ref[0] = mlhs[0, :, :rows].astype(jnp.float32).reshape(2, virt, rows)

        def adjoint_tile(j, c):
            columns = pl.ds(pl.multiple_of(j * TILE, TILE), TILE)
            out = None
            for p in range(2):
                term = jnp.dot(
                    mlhs[p, :, :rows], refl[p, :, columns], preferred_element_type=jnp.float32
                )
                out = term if out is None else out + term
            acc[:, columns] = out.astype(jnp.bfloat16)
            return c

        lax.fori_loop(0, points // TILE, adjoint_tile, 0)
        for k in range(n_src):
            at = wide_starts[k]
            part_snd[k] = acc[:, at : at + wide]
        exchange(2, "src", n_src, me_s, lambda k: part_snd.at[k], got3)
        total = got3[0].astype(jnp.float32)
        for k in range(1, n_src):
            total = total + got3[k].astype(jnp.float32)
        low = total.astype(jnp.bfloat16)
        for k in range(n_freq):
            at = narrow_starts[k]
            snd[k] = low[:, at : at + narrow]
        exchange(3, "freq", n_freq, me_f, lambda k: snd.at[k], got4)
        window(got4, onset_recv_ref, snd)
        exchange(4, "freq", n_freq, me_f, lambda k: snd.at[k], got5)
        for k in range(n_freq):
            at = narrow_starts[k]
            piece[:, at : at + narrow] = got5[k]
        exchange(5, "src", n_src, me_s, lambda k: piece, got6)
        for k in range(n_src):
            at = wide_starts[k]
            zero = zero_ref[0, :, :, at : at + wide].reshape(two_v, wide)
            plus = zero + got6[k].astype(jnp.float32)
            plus_ref[0, :, :, at : at + wide] = plus.reshape(2, virt, wide)
            lhs[0, :, at : at + wide] = plus.astype(jnp.bfloat16)
            lhs[1, :virt, at : at + wide] = (-plus[virt:]).astype(jnp.bfloat16)
            lhs[1, virt:, at : at + wide] = plus[:virt].astype(jnp.bfloat16)
        return carry

    lax.fori_loop(0, ROUNDS, round_body, 0)


def body(reflection, f_zero, onset):
    n_freq = lax.axis_size("freq")
    n_src = lax.axis_size("src")
    freq_index = lax.axis_index("freq")
    src_index = lax.axis_index("src")
    _, _, rows, points = reflection.shape
    virt = f_zero.shape[2]
    two_v = 2 * virt
    wide = round_up(rows, LANES)
    narrow = round_up(-(-wide // n_freq), LANES)
    narrow_start = jnp.minimum(freq_index * narrow, wide - narrow)
    own = lax.dynamic_slice_in_dim(onset, src_index * rows, rows, 1)
    onset_src = lax.dynamic_slice_in_dim(
        jnp.pad(own, ((0, 0), (0, wide - rows))), narrow_start, narrow, 1
    )
    onset_recv = lax.dynamic_slice_in_dim(
        onset, jnp.minimum(src_index * wide, points - wide) + narrow_start, narrow, 1
    )
    table = np.repeat(band_table(n_freq), virt, axis=0).astype(ml_dtypes.bfloat16)
    gather = jnp.asarray(table)
    spread = jnp.asarray(np.ascontiguousarray(table.T))
    low = jnp.bfloat16
    vmem = pl.BlockSpec(memory_space=pltpu.VMEM)
    exchange_shape = pltpu.VMEM((n_freq, two_v, narrow), low)
    piece_shape = pltpu.VMEM((n_src, two_v, wide), low)
    return pl.pallas_call(
        functools.partial(kernel, n_freq, n_src),
        out_shape=(
            jax.ShapeDtypeStruct(f_zero.shape, jnp.float32),
            jax.ShapeDtypeStruct((1, 2, virt, rows), jnp.float32),
        ),
        in_specs=[pl.BlockSpec(memory_space=pl.ANY)] + [vmem] * 5,
        out_specs=(vmem, vmem),
        scratch_shapes=[
            pltpu.VMEM((2, rows, points), low),
            pltpu.VMEM((2, two_v, points), low),
            pltpu.VMEM((2, two_v, wide), low),
            pltpu.VMEM((two_v, wide), jnp.float32),
            pltpu.VMEM((two_v, points), low),
            exchange_shape,
            exchange_shape,
            exchange_shape,
            piece_shape,
            piece_shape,
            exchange_shape,
            exchange_shape,
            pltpu.VMEM((two_v, wide), low),
            piece_shape,
            pltpu.SemaphoreType.DMA((-(-rows // TILE),)),
            pltpu.SemaphoreType.DMA((6, max(n_freq, n_src))),
            pltpu.SemaphoreType.DMA((6, max(n_freq, n_src))),
        ],
        compiler_params=pltpu.CompilerParams(
            collective_id=0, has_side_effects=True, vmem_limit_bytes=60 * 2**20
        ),
    )(reflection, f_zero, onset_src, onset_recv, spread, gather)


def solution(mesh):
    return jax.shard_map(
        body,
        mesh=mesh,
        in_specs=(P("freq", None, "src", None), P("freq", None, None, None), P()),
        out_specs=(P("freq", None, None, None), P("freq", None, None, "src")),
        check_vma=False,
    )
```

time: 1370 us -> 336 us (0.25)
  matrix products: 487 us -> 0 us
  Pallas kernels: 0 us -> 329 us
  blocking collectives: 301 us -> 0 us
  waiting for transfers between devices: 266 us -> 0 us
  local copies, waits for them, and re-layouts: 255 us -> 6.15 us
  other arithmetic: 24.4 us -> 0 us
  starting transfers between devices: 14.7 us -> 0 us
  between operations: 15 us -> 0.66 us
    dot_general x30 -> x0, matrix products: 487 us -> none  [the longest x10 164 us: windowed(): jnp.einsum('an,at->nt', flat, table, precision=lax.Precision.HIGHEST)]
    pallas_call x0 -> x1, Pallas kernels: none -> 329 us  [body(): pl.pallas_call(functools.partial(kernel, n_freq, n_src), out_shape=(jax.S...]
    all_to_all x17 -> x0, blocking collectives: 301 us -> none  [the longest x4 106 us: body(): lax.all_to_all(windowed(cut_total, onset_recv, table), 'freq', split_axis...]
    psum x5 -> x0, waiting for transfers between devices: 214 us -> none  [body(): lax.psum(partial_sum.astype(jnp.bfloat16), 'src').astype(jnp.float32)]
    unnamed x26 -> x2, local copies, waits for them, and re-layouts: 133 us -> 3.72 us
    all_to_all x26 -> x0, local copies, waits for them, and re-layouts: 67.6 us -> none  [the longest x5 43.7 us: body(): lax.all_to_all(total, 'freq', split_axis=3, concat_axis=0, tiled=True)]
    all_to_all x3 -> x0, waiting for transfers between devices: 52.1 us -> none  [the longest x1 22.7 us: body(): lax.all_to_all(windowed(cut_total, onset_recv, table), 'freq', split_axis...]
    convert_element_type x12 -> x0, local copies, waits for them, and re-layouts: 37 us -> none  [the longest x5 35.8 us: body(): lax.psum(partial_sum.astype(jnp.bfloat16), 'src').astype(jnp.float32)]
  transfers between devices with their start and end apart: 8 -> 0, of which waited for: 8 -> 0; matrix products, arithmetic and copies ran while one was open for 0% -> 0% of each run, Pallas kernels for 0% -> 0%
where the time goes in v1:
time: 336 us
  Pallas kernels  329 us (98%)
  local copies, waits for them, and re-layouts  6.15 us (2%)
    pallas_call x1, Pallas kernels, body(): pl.pallas_call(functools.partial(kernel, n_freq, n_src), out_shape=(jax.S...  329 us

profile of v1, /device:TPU:0, one launch (start us, length us, event | category | flops | bytes accessed | tf_op | source)
XLA Modules:
  0.0 335.9 jit_solution(4869915700549563915)
XLA Ops:
  0.6 1.0 constant_dynamic-slice_fusion.1
  1.6 1.4 pad_dynamic-slice_fusion
  3.1 329.0 %shard_map.68 = (f32[1,2,16,6400]{3,2,1,0:T(8,128)}, f32[1,2,16,1600]{3,2,1,0:T(8,128)}) custom-call(bf16[1,2,1600,6400]{3,2,1,0:T(8,128)(2,1)} %refl_hbm.1, f32[1,2,16,6400]{3,2,1,0:T(8,128)} %zero_ref.1, s32[16,256]{1,0:T(8,128)} %get-tuple-element.2.onset_src_ref, s32[16,256]{1,0:T(8,128)} %get-tuple-element.3.onset_recv_ref, ...), custom_call_target="tpu_custom_call" | custom-call | tf_op jit(solution)/shard_map/pallas_call | solution.py:262
  332.1 2.1 copy.9
  334.2 1.6 copy.10

commit v2 on v1

--- a/solution.py
+++ b/solution.py
@@ -51,7 +51,6 @@
     lhs,
     mlhs,
     rec,
-    acc,
     snd,
     got1,
     got2,
@@ -129,7 +128,7 @@
             return jnp.where(mine, back, total)
 
         total = lax.fori_loop(
-            0, virt, one, jnp.zeros((n_freq * two_v, narrow), jnp.float32), unroll=2
+            0, virt, one, jnp.zeros((n_freq * two_v, narrow), jnp.float32), unroll=16
         )
         target[...] = total.astype(jnp.bfloat16).reshape(n_freq, two_v, narrow)
 
@@ -146,16 +145,35 @@
         out = None
         for p in range(2):
             term = lax.dot_general(
+                refl[p, pl.ds(start, size), :],
                 lhs[p],
-                refl[p, pl.ds(start, size), :],
                 (((1,), (1,)), ((), ())),
                 preferred_element_type=jnp.float32,
             )
             out = term if out is None else out + term
-        return out
+        return out.T
 
     def round_body(step, carry):
         full = rows // TILE
+
+        def to_freq(k, slot):
+            return pltpu.make_async_remote_copy(
+                src_ref=snd.at[k],
+                dst_ref=got1.at[slot],
+                send_sem=send_sem.at[0, k],
+                recv_sem=recv_sem.at[0, slot],
+                device_id={"freq": k},
+                device_id_type=MESH,
+            )
+
+        def send_records(k, block):
+            snd[k] = block.astype(jnp.bfloat16)
+
+            @pl.when(k != me_f)
+            def _():
+                to_freq(k, me_f).start()
+
+        each = TILE // narrow
 
         def forward_tile(j, c):
             start = pl.multiple_of(j * TILE, TILE)
@@ -164,7 +182,10 @@
             def _():
                 load(j, start, TILE).wait()
 
-            rec[:, pl.ds(start, TILE)] = forward(start, TILE)
+            out = forward(start, TILE)
+            rec[:, pl.ds(start, TILE)] = out
+            for i in range(each):
+                send_records(j * each + i, out[:, i * narrow : (i + 1) * narrow])
             return c
 
         lax.fori_loop(0, full, forward_tile, 0)
@@ -176,10 +197,13 @@
                 load(full, start, size).wait()
 
             rec[:, start : start + size] = forward(start, size)
-        for k in range(n_freq):
+        for k in range(full * each, n_freq):
             at = narrow_starts[k]
-            snd[k] = rec[:, at : at + narrow].astype(jnp.bfloat16)
-        exchange(0, "freq", n_freq, me_f, lambda k: snd.at[k], got1)
+            send_records(k, rec[:, at : at + narrow])
+        got1[me_f] = snd[me_f]
+        for d in range(1, n_freq):
+            k = lax.rem(me_f + d, n_freq)
+            to_freq(k, k).wait()
         window(got1, onset_src_ref, snd)
         exchange(1, "freq", n_freq, me_f, lambda k: snd.at[k], got2)
         for k in range(n_freq):
@@ -191,22 +215,41 @@
             mlhs[1, virt:, at : at + narrow] = (-value[:virt]).astype(jnp.bfloat16)
         minus_ref[0] = mlhs[0, :, :rows].astype(jnp.float32).reshape(2, virt, rows)
 
-        def adjoint_tile(j, c):
-            columns = pl.ds(pl.multiple_of(j * TILE, TILE), TILE)
+        def to_src(d):
+            peer = lax.rem(me_s + d, n_src)
+            return pltpu.make_async_remote_copy(
+                src_ref=part_snd.at[peer],
+                dst_ref=got3.at[me_s],
+                send_sem=send_sem.at[2, d],
+                recv_sem=recv_sem.at[2, d],
+                device_id={"src": peer},
+                device_id_type=MESH,
+            )
+
+        def adjoint(peer):
+            start = peer * wide - (peer // (n_src - 1)) * (n_src * wide - points)
+            columns = pl.ds(pl.multiple_of(start, LANES), wide)
             out = None
             for p in range(2):
                 term = jnp.dot(
                     mlhs[p, :, :rows], refl[p, :, columns], preferred_element_type=jnp.float32
                 )
                 out = term if out is None else out + term
-            acc[:, columns] = out.astype(jnp.bfloat16)
+            part_snd[peer] = out.astype(jnp.bfloat16)
+
+        def adjoint_piece(d, c):
+            adjoint(lax.rem(me_s + d, n_src))
+
+            @pl.when(d < n_src)
+            def _():
+                to_src(d).start()
+
             return c
 
-        lax.fori_loop(0, points // TILE, adjoint_tile, 0)
-        for k in range(n_src):
-            at = wide_starts[k]
-            part_snd[k] = acc[:, at : at + wide]
-        exchange(2, "src", n_src, me_s, lambda k: part_snd.at[k], got3)
+        lax.fori_loop(1, n_src + 1, adjoint_piece, 0)
+        got3[me_s] = part_snd[me_s]
+        for d in range(1, n_src):
+            to_src(d).wait()
         total = got3[0].astype(jnp.float32)
         for k in range(1, n_src):
             total = total + got3[k].astype(jnp.float32)
@@ -272,7 +315,6 @@
             pltpu.VMEM((2, two_v, points), low),
             pltpu.VMEM((2, two_v, wide), low),
             pltpu.VMEM((two_v, wide), jnp.float32),
-            pltpu.VMEM((two_v, points), low),
             exchange_shape,
             exchange_shape,
             exchange_shape,

time: 336 us -> 268 us (0.80)
  Pallas kernels: 329 us -> 261 us
    pallas_call x1, Pallas kernels: 329 us -> 261 us  [body(): pl.pallas_call(functools.partial(kernel, n_freq, n_src), out_shape=(jax.S...]
where the time goes in v2:
time: 268 us
  Pallas kernels  261 us (97%)
  local copies, waits for them, and re-layouts  6.15 us (2%)
    pallas_call x1, Pallas kernels, body(): pl.pallas_call(functools.partial(kernel, n_freq, n_src), out_shape=(jax.S...  261 us

profile of v2, /device:TPU:0, one launch (start us, length us, event | category | flops | bytes accessed | tf_op | source)
XLA Modules:
  0.0 267.6 jit_solution(4758257126185064020)
XLA Ops:
  0.6 1.0 constant_dynamic-slice_fusion.1
  1.6 1.4 pad_dynamic-slice_fusion
  3.1 260.8 %shard_map.68 = (f32[1,2,16,6400]{3,2,1,0:T(8,128)}, f32[1,2,16,1600]{3,2,1,0:T(8,128)}) custom-call(bf16[1,2,1600,6400]{3,2,1,0:T(8,128)(2,1)} %refl_hbm.1, f32[1,2,16,6400]{3,2,1,0:T(8,128)} %zero_ref.1, s32[16,256]{1,0:T(8,128)} %get-tuple-element.2.onset_src_ref, s32[16,256]{1,0:T(8,128)} %get-tuple-element.3.onset_recv_ref, ...), custom_call_target="tpu_custom_call" | custom-call | tf_op jit(solution)/shard_map/pallas_call | solution.py:305
  263.9 2.1 copy.9
  266.0 1.6 copy.10
